TPU v7x, 256 devices: a whole 4x4x8 slice. The times are simulated.
256 devices in a mesh: dp: 2 (over core), seq: 16 (over z_lo, x), chan: 8 (over y, z_hi).
Axes of the slice: x: 4, y: 4, z: 8 (z_hi: 2, z_lo: 4; z = z_hi * 4 + z_lo), core: 2. Of those that a mesh axis runs over, the one named last changes fastest.
Arguments:
- tokens: bfloat16 [1, 8192, 4096], P(None, ('dp', 'seq'), 'chan'), may hold values from -6 to 6
- w_value: bfloat16 [4096, 4096], P(None, 'chan'), may hold values from -0.09375 to 0.09375
- gate_k: bfloat16 [1, 8192, 4096], P(None, ('dp', 'seq'), 'chan'), may hold values from -5 to 5
- gate_q: bfloat16 [1, 8192, 4096], P(None, ('dp', 'seq'), 'chan'), may hold values from -5 to 5
- filter_weight: float32 [64, 4096], P(None, 'chan'), may hold values from -6 to 6
- decay: float32 [4096], P('chan'), may hold values from 0.5 to 8
- skip_bias: float32 [4096], P('chan'), may hold values from 0.5 to 1.5
- cotangent: bfloat16 [1, 8192, 4096], P(None, ('dp', 'seq'), 'chan'), may hold values from -16 to 16
Outputs:
- mixed: bfloat16 [1, 8192, 4096], P(None, ('dp', 'seq'), 'chan')
- grad_tokens: bfloat16 [1, 8192, 4096], P(None, ('dp', 'seq'), 'chan')
- grad_gate_k: bfloat16 [1, 8192, 4096], P(None, ('dp', 'seq'), 'chan')
- grad_gate_q: bfloat16 [1, 8192, 4096], P(None, ('dp', 'seq'), 'chan')
- grad_filter: float32 [64, 4096], P(None, 'chan')
- grad_bias: float32 [4096], P('chan')
All inputs are finite; a program needn't handle non-finite values.
Results may differ from a plain program's by a relative error of at most 0.012.
Values may be sent and summed in bfloat16 or wider, within the bound.
A program may use at most 128 MiB of HBM per device.

v0:
```python
import math

import jax
import jax.numpy as jnp
import numpy as np
from jax import lax
from jax.sharding import PartitionSpec as P

BF = jnp.bfloat16
F32 = jnp.float32


def tables(block, order):
    pos = np.arange(block, dtype=np.float64)
    harm = 2.0 * np.pi / block * np.arange(1, order + 1, dtype=np.float64)
    half = np.pi / block * (2.0 * np.arange(block // 2, dtype=np.float64) + 1.0)
    even = harm[:, None] * pos[None, :]
    odd = half[:, None] * pos[None, :]
    dft = np.concatenate([np.cos(even), np.sin(even), np.cos(odd), np.sin(odd)])
    cross = np.sin(odd) @ np.cos(even).T
    return dft.astype(np.float32), cross.astype(np.float32)


def dot(a, b):
    return jnp.dot(a.astype(BF), b.astype(BF), preferred_element_type=F32)


def body(tokens, w_value, gate_k, gate_q, filter_weight, decay, skip_bias, cotangent):
    tok = tokens[0]
    block, width = tok.shape
    groups = lax.axis_size(("dp", "seq"))
    index = lax.axis_index(("dp", "seq"))
    length = block * groups
    order = filter_weight.shape[0]
    scale = 1.0 / math.sqrt(order * length)
    dft_np, cross_np = tables(block, order)
    dft = jnp.asarray(dft_np)
    cross = jnp.asarray(cross_np)
    n_even = 2 * order
    half = block // 2
    values = jnp.dot(
        lax.all_gather(tok, "chan", axis=1, tiled=True), w_value, preferred_element_type=F32
    ).astype(BF).astype(F32)
    key = gate_k[0].astype(F32)
    query = gate_q[0].astype(F32)
    inc = cotangent[0].astype(F32)
    mixed_in = key * values
    grad_state = query * inc
    pos = jnp.arange(block, dtype=F32)[:, None] / length
    fade = jnp.exp(-pos * decay[None, :])
    grow = jnp.exp(pos * decay[None, :])
    x_spec = dot(dft, mixed_in * grow)
    g_spec = dot(dft, grad_state * fade)
    weights = filter_weight * scale
    kern_c = jnp.sum(weights, axis=0, keepdims=True)
    kern_s = jnp.dot(cross, weights, precision=lax.Precision.HIGHEST)

    states = jnp.concatenate([x_spec[:n_even], g_spec[:n_even]])
    sub = width // groups
    mine = lax.all_to_all(
        states.reshape(2 * n_even, groups, sub), ("dp", "seq"), split_axis=1, concat_axis=1, tiled=True
    )
    dec = lax.dynamic_slice_in_dim(decay, index * sub, sub, 0)
    ids = jnp.arange(groups)
    gap = (ids[:, None] - ids[None, :]).astype(F32)
    low = jnp.where(
        gap[:, :, None] > 0, jnp.exp(-jnp.maximum(gap, 0.0)[:, :, None] * dec * (block / length)), 0.0
    )
    carried_x = jnp.einsum("ijc,rjc->ric", low, mine[:n_even], precision=lax.Precision.HIGHEST)
    carried_g = jnp.einsum("jic,rjc->ric", low, mine[n_even:], precision=lax.Precision.HIGHEST)
    back = lax.all_to_all(
        jnp.concatenate([carried_x, carried_g]), ("dp", "seq"), split_axis=1, concat_axis=1, tiled=True
    ).reshape(2 * n_even, width)
    z_x, z_g = back[:n_even], back[n_even:]

    two = jnp.concatenate([weights, weights])
    xe, ge = x_spec[:n_even], g_spec[:n_even]
    xc, xs = x_spec[n_even : n_even + half], x_spec[n_even + half :]
    gc, gs = g_spec[n_even : n_even + half], g_spec[n_even + half :]
    inv = 1.0 / block
    y_spec = jnp.concatenate(
        [two * (z_x + 0.5 * xe), inv * (kern_c * xc - kern_s * xs), inv * (kern_c * xs + kern_s * xc)]
    )
    p_spec = jnp.concatenate(
        [two * (z_g + 0.5 * ge), inv * (kern_c * gc + kern_s * gs), inv * (kern_c * gs - kern_s * gc)]
    )
    gated_state = fade * dot(dft.T, y_spec) + skip_bias * mixed_in
    grad_in = grow * dot(dft.T, p_spec) + skip_bias * grad_state

    n_c = gc * xc + gs * xs
    n_s = gs * xc - gc * xs
    prod = ge * (z_x + 0.5 * xe)
    part = scale * (
        prod[:order]
        + prod[order:]
        + inv * (jnp.sum(n_c, axis=0, keepdims=True) + jnp.dot(cross.T, n_s, precision=lax.Precision.HIGHEST))
    )
    part_bias = jnp.sum(mixed_in * grad_state, axis=0, keepdims=True)
    sums = lax.psum(jnp.concatenate([part, part_bias]), ("dp", "seq"))

    mixed = (query * gated_state).astype(BF)
    grad_values = (key * grad_in).astype(BF)
    terms = lax.dot_general(
        grad_values, w_value, (((1,), (1,)), ((), ())), preferred_element_type=F32
    )
    grad_tok = lax.psum_scatter(terms, "chan", scatter_dimension=1, tiled=True).astype(BF)
    grad_key = (values * grad_in).astype(BF)
    grad_query = (gated_state * inc).astype(BF)
    return (
        mixed[None],
        grad_tok[None],
        grad_key[None],
        grad_query[None],
        sums[:order],
        sums[order],
    )


def solution(mesh):
    rows = P(None, ("dp", "seq"), "chan")
    cols = P(None, "chan")
    return jax.shard_map(
        body,
        mesh=mesh,
        in_specs=(rows, cols, rows, rows, cols, P("chan"), P("chan"), rows),
        out_specs=(rows, rows, rows, rows, cols, P("chan")),
        check_vma=False,
    )
```

profile of v0, /device:TPU:64, one launch (start us, length us, event | category | flops | bytes accessed | tf_op | source)
XLA Modules:
  0.0 543.2 jit_solution(2549810589941749096)
XLA Ops:
  7.2 0.7 all-gather.3.cloned.1.call-update
  7.9 1.5 fusion.20
  9.5 77.8 %all-gather.3.cloned.1.call-done = bf16[1,256,4096]{2,1,0:T(8,128)(2,1)} async-done(((bf16[1,256,512]{2,1,0:T(8,128)(2,1)}), bf16[1,256,4096]{2,1,0:T(8,128)(2,1)}) %all-gather.3.cloned.1.call-update) | async-done | bytes 2097168 | tf_op jit(solution)/shard_map/all_gather | solution.py:42
  87.3 4.1 fusion.9
  91.4 0.4 fusion.19
  91.9 1.0 copy.27
  92.9 7.6 %all-to-all-start = ((f32[256,32,16]{0,2,1:T(8,128)}), f32[256,32,16]{0,2,1:T(8,128)S(1)}, u32[]{:S(2)}, u32[]{:S(2)}) async-start(f32[256,32,16]{0,2,1:T(8,128)} %bitcast.5), calls=%async_computation | async-start | bytes 1048576 | tf_op jit(solution)/shard_map/all_to_all | solution.py:60
  100.6 14.1 %all-to-all-done = f32[256,32,16]{0,2,1:T(8,128)S(1)} async-done(((f32[256,32,16]{0,2,1:T(8,128)}), f32[256,32,16]{0,2,1:T(8,128)S(1)}, u32[]{:S(2)}, u32[]{:S(2)}) %all-to-all-start) | async-done | bytes 524320 | tf_op jit(solution)/shard_map/all_to_all | solution.py:60
  114.7 0.7 convolution_bitcast_fusion.1
  115.4 0.5 convolution_bitcast_fusion
  115.9 1.1 copy.31
  117.0 6.8 %all-to-all-start.1 = ((f32[256,32,16]{0,2,1:T(8,128)}), f32[256,32,16]{0,2,1:T(8,128)S(1)}, u32[]{:S(2)}, u32[]{:S(2)}) async-start(f32[256,32,16]{0,2,1:T(8,128)} %copy.31), calls=%async_computation.1 | async-start | bytes 1048576 | tf_op jit(solution)/shard_map/all_to_all | solution.py:71
  123.9 0.4 fusion.83
  124.3 13.8 %all-to-all-done.1 = f32[256,32,16]{0,2,1:T(8,128)S(1)} async-done(((f32[256,32,16]{0,2,1:T(8,128)}), f32[256,32,16]{0,2,1:T(8,128)S(1)}, u32[]{:S(2)}, u32[]{:S(2)}) %all-to-all-start.1) | async-done | bytes 524320 | tf_op jit(solution)/shard_map/all_to_all | solution.py:71
  138.1 0.7 fusion.87
  138.8 1.1 copy.33
  139.9 0.1 copy.32
  140.1 0.2 add_reduce_fusion
  140.3 1.1 fusion.48
  141.4 1.1 fusion.46
  142.5 0.2 convolution_add_fusion.1
  142.8 0.2 convolution_add_fusion.3
  143.0 0.3 fusion.15
  143.4 0.3 fusion.5
  143.7 1.3 fusion.22
  145.0 0.7 pad_maximum_fusion.3
  145.8 5.4 fusion.23
  151.2 252.3 %all-reduce.2.cloned.1.call-done = f32[65,512]{1,0:T(8,128)} async-done(((f32[65,512]{1,0:T(8,128)}), f32[65,512]{1,0:T(8,128)}) %all-reduce.2.cloned.1.call-update) | async-done | bytes 133136 | tf_op jit(solution)/shard_map/psum | solution.py:99
  403.6 1.3 slice.85
  404.9 1.6 slice.84
  406.4 128.5 %reduce-scatter.2.cloned.1.call-done = f32[256,512]{1,0:T(8,128)} async-done(((f32[256,4096]{1,0:T(8,128)}), f32[256,512]{1,0:T(8,128)}) %reduce-scatter.2.cloned.1.call-update) | async-done | bytes 524304 | tf_op jit(solution)/shard_map/reduce_scatter | solution.py:106
  534.9 1.8 convert_bitcast_fusion
  (38 shorter events, 0.5 us)
Async XLA Ops:
  7.2 80.1 %all-gather.3.cloned.1.call-start = ((), (), s32[]{:S(2)}) async-start(), calls=%async_computation.5 | async-start | bytes 2359296 | tf_op jit(solution)/shard_map/all_gather | solution.py:42
  9.4 81.9 %copy-start.2 = (bf16[1,256,512]{2,1,0:T(8,128)(2,1)S(1)}, bf16[1,256,512]{2,1,0:T(8,128)(2,1)}, u32[]{:S(2)}) copy-start(bf16[1,256,512]{2,1,0:T(8,128)(2,1)} %param.12) | copy-start | bytes 786436
  9.4 81.9 %copy-start.3 = (bf16[384,256]{1,0:T(8,128)(2,1)S(1)}, bf16[384,256]{1,0:T(8,128)(2,1)}, u32[]{:S(2)}) copy-start(bf16[384,256]{1,0:T(8,128)(2,1)} %constant.40) | copy-start | bytes 589828
  9.5 81.9 %copy-start.9 = (f32[512]{0:T(512)S(1)}, f32[512]{0:T(512)}, u32[]{:S(2)}) copy-start(f32[512]{0:T(512)} %param.15) | copy-start | bytes 6148
  91.8 32.1 %copy-start.4 = (f32[64,512]{1,0:T(8,128)S(1)}, f32[64,512]{1,0:T(8,128)}, u32[]{:S(2)}) copy-start(f32[64,512]{1,0:T(8,128)} %param.14) | copy-start | bytes 393220
  91.8 32.1 %copy-start.7 = (f32[128,64]{1,0:T(8,128)S(1)}, f32[128,64]{1,0:T(8,128)}, u32[]{:S(2)}) copy-start(f32[128,64]{1,0:T(8,128)} %constant.39.clone) | copy-start | bytes 98308
  92.9 21.8 %all-to-all-start = ((f32[256,32,16]{0,2,1:T(8,128)}), f32[256,32,16]{0,2,1:T(8,128)S(1)}, u32[]{:S(2)}, u32[]{:S(2)}) async-start(f32[256,32,16]{0,2,1:T(8,128)} %bitcast.5), calls=%async_computation | async-start | bytes 1048576 | tf_op jit(solution)/shard_map/all_to_all | solution.py:60
  117.0 21.0 %all-to-all-start.1 = ((f32[256,32,16]{0,2,1:T(8,128)}), f32[256,32,16]{0,2,1:T(8,128)S(1)}, u32[]{:S(2)}, u32[]{:S(2)}) async-start(f32[256,32,16]{0,2,1:T(8,128)} %copy.31), calls=%async_computation.1 | async-start | bytes 1048576 | tf_op jit(solution)/shard_map/all_to_all | solution.py:71
  123.8 279.7 %all-reduce.2.cloned.1.call-start = ((), (), s32[]{:S(2)}) async-start(), calls=%async_computation.4 | async-start | bytes 294912 | tf_op jit(solution)/shard_map/psum | solution.py:99
  140.0 2.5 copy-start.6
  140.0 3.0 copy-start.8
  140.1 3.3 copy-start
  140.1 3.3 copy-start.1
  140.1 3.3 copy-start.5
  140.1 3.3 copy-start.10
  145.7 389.2 %reduce-scatter.2.cloned.1.call-start = ((), (), s32[]{:S(2)}) async-start(), calls=%async_computation.3 | async-start | bytes 4718592 | tf_op jit(solution)/shard_map/reduce_scatter | solution.py:106
Sparse Core Ops, SparseCore 0:
  10.5 76.7 all-gather.2
  145.9 257.6 all-reduce.1
  408.3 126.5 reduce-scatter.1
where the time goes:
time: 546 us; the launch traced here: 543 us
  waiting for transfers between devices  487 us (89%)
  matrix products  17.5 us (3%)
  starting transfers between devices  14.5 us (3%)
  between operations  14.1 us (3%)
  local copies, waits for them, and re-layouts  7.12 us (1%)
    psum x1, waiting for transfers between devices, body(): sums = lax.psum(jnp.concatenate([part, part_bias]), ('dp', 'seq'))  252 us
    reduce_scatter x1, waiting for transfers between devices, body(): lax.psum_scatter(terms, 'chan', scatter_dimension=1, tiled=True).astype(BF)  128 us
    all_gather x1, waiting for transfers between devices, body(): lax.all_gather(tok, 'chan', axis=1, tiled=True)  77.8 us
    all_to_all x1, waiting for transfers between devices, body(): lax.all_to_all(states.reshape(2 * n_even, groups, sub), ('dp', 'seq'), sp...  14.1 us
    all_to_all x1, waiting for transfers between devices, body(): lax.all_to_all(jnp.concatenate([carried_x, carried_g]), ('dp', 'seq'), sp...  13.8 us
  transfers between devices with their start and end apart: 5, of which 5 were waited for; matrix products, arithmetic and copies ran while one was open for 2% of the time, Pallas kernels for 0%

commit v1 on v0

v1 whole, which is shorter than its diff:
```python
import functools
import math

import jax
import jax.numpy as jnp
import numpy as np
from jax import lax
from jax.experimental import pallas as pl
from jax.experimental.pallas import tpu as pltpu
from jax.sharding import PartitionSpec as P

BF = jnp.bfloat16
F32 = jnp.float32
MESH = pl.DeviceIdType.MESH
EXACT = lax.Precision.HIGHEST
NT = (((1,), (1,)), ((), ()))


def tables(block, order):
    pos = np.arange(block, dtype=np.float64)
    harm = 2.0 * np.pi / block * np.arange(1, order + 1, dtype=np.float64)
    half = np.pi / block * (2.0 * np.arange(block // 2, dtype=np.float64) + 1.0)
    even = harm[:, None] * pos[None, :]
    odd = half[:, None] * pos[None, :]
    pair = np.stack([np.cos(even).reshape(-1, 8, block), np.sin(even).reshape(-1, 8, block)], 1)
    dft = np.concatenate([pair.reshape(2 * order, block), np.cos(odd), np.sin(odd)])
    cross = np.sin(odd) @ np.cos(even).T
    return dft.astype(np.float32), cross.astype(np.float32)


def mm(a, b):
    return jnp.dot(a, b, preferred_element_type=F32)


def kernel(
    seq_size, length,
    tok_h, w_h, gk_h, gq_h, fw_h, cot_h, dft_h, idft_h, cross_h, crosst_h, dec, bias,
    mixed_o, gtok_o, gkey_o, gqry_o, gf_o, gb_o,
    tok, w, gk, gq, fw, cot, dft, idft, cross, crosst,
    fade, grow, gs, gin, xin, val, gval, acc, gspec, xspec, pspec, kern, wts, carry,
    src, dst, terms, send_a, send_p, send_s, send_z, got_a, got_b, got_z,
    load_sem, ag_send, ag_recv, rs_send, rs_recv, st_send, st_recv,
):
    block, width = gk.shape
    rows = block // 2
    order = fw.shape[0]
    groups = 2 * seq_size
    n_even = 2 * order
    half = block // 2
    lanes = src.shape[3]
    n_rg = n_even // 16
    n_cg = width // lanes
    scale = 1.0 / math.sqrt(order * length)
    inv = 1.0 / block

    dp, seq, chan = lax.axis_index("dp"), lax.axis_index("seq"), lax.axis_index("chan")
    me = dp * seq_size + seq
    y, zh = chan // 2, chan % 2

    def chan_at(dy, other):
        return ((y + dy) % 4) * 2 + (zh + other) % 2

    def at_chan(c):
        return (dp, seq, c)

    up, down, across = at_chan(chan_at(1, 0)), at_chan(chan_at(3, 0)), at_chan(chan_at(0, 1))

    def peer(i):
        b = (me + i) % groups
        return b, (b // seq_size, b % seq_size, chan)

    loads = {}
    order_of = [
        ("gq", gq_h, gq), ("cot", cot_h, cot), ("dft", dft_h, dft), ("fw", fw_h, fw), ("cross", cross_h, cross),
        ("gk", gk_h, gk), ("idft", idft_h, idft), ("crosst", crosst_h, crosst), ("w", w_h, w),
        ("tok", tok_h, tok.at[chan]),
    ]
    for i, (name, a, b) in enumerate(order_of):
        loads[name] = pltpu.make_async_copy(a, b, load_sem.at[i])
        loads[name].start()

    barrier = pltpu.get_barrier_semaphore()
    for target in (up, down, across):
        pl.semaphore_signal(barrier, inc=1, device_id=target, device_id_type=MESH)

    def greet(i, carry_):
        pl.semaphore_signal(barrier, inc=1, device_id=peer(i)[1], device_id_type=MESH)
        return carry_

    lax.fori_loop(1, groups, greet, 0)
    pl.semaphore_wait(barrier, groups + 2)

    top, bot = pl.ds(0, rows), pl.ds(rows, rows)

    ag = []

    def gather(i, slot, part, target, first=False):
        s = tok_h.at[part] if first else tok.at[slot, part]
        cp = pltpu.make_async_remote_copy(
            src_ref=s, dst_ref=tok.at[slot, part], send_sem=ag_send.at[i], recv_sem=ag_recv.at[i],
            device_id=target, device_id_type=MESH,
        )
        cp.start()
        ag.append(cp)

    def arrived(i, slot, part):
        r = tok.at[slot, part]
        pltpu.make_async_copy(r, r, ag_recv.at[i]).wait()

    gather(0, chan, top, across, True)
    gather(2, chan, top, up, True)
    gather(4, chan, bot, down, True)
    gather(1, chan, bot, across, True)
    gather(3, chan, bot, up, True)
    gather(5, chan, top, down, True)

    def spread(trip, single=False):
        def one(i, carry_):
            b, target = peer(i)
            s = src.at[trip, 0] if single else src.at[trip, b]
            pltpu.make_async_remote_copy(
                src_ref=s, dst_ref=dst.at[trip, me], send_sem=st_send.at[trip], recv_sem=st_recv.at[trip],
                device_id=target, device_id_type=MESH,
            ).start()
            return carry_

        lax.fori_loop(1, groups, one, 0, unroll=True)
        dst[trip, me] = src[trip, 0] if single else src[trip, me]

    def landed(trip):
        r = dst.at[trip, pl.ds(0, groups - 1)]
        pltpu.make_async_copy(r, r, st_recv.at[trip]).wait()

    def left(trip):
        r = src.at[trip, pl.ds(0, groups - 1)]
        pltpu.make_async_copy(r, r, st_send.at[trip]).wait()

    def stage(trip, ref):
        for rg in range(n_rg):
            for cg in range(n_cg):
                src[trip, rg * n_cg + cg] = ref[pl.ds(16 * rg, 16), pl.ds(lanes * cg, lanes)].astype(BF)

    def unstage(trip):
        for rg in range(n_rg):
            for cg in range(n_cg):
                carry[pl.ds(16 * rg, 16), pl.ds(lanes * cg, lanes)] = dst[trip, rg * n_cg + cg].astype(F32)

    loads["gq"].wait()
    loads["cot"].wait()
    pos = lax.broadcasted_iota(jnp.int32, (block, width), 0).astype(F32) * (1.0 / length)
    rate = pos * dec[...]
    fade[...] = jnp.exp(-rate)
    grow[...] = jnp.exp(rate)
    gs[...] = gq[...].astype(F32) * cot[...].astype(F32)
    loads["dft"].wait()
    gspec[...] = mm(dft[...], (gs[...] * fade[...]).astype(BF))
    stage(0, gspec)
    spread(0)

    loads["fw"].wait()
    loads["cross"].wait()
    scaled = fw[...] * scale
    for rg in range(n_rg):
        eight = scaled[8 * rg : 8 * rg + 8]
        wts[pl.ds(16 * rg, 8), :] = eight
        wts[pl.ds(16 * rg + 8, 8), :] = eight
    kern[...] = jnp.dot(cross[...], scaled, precision=EXACT, preferred_element_type=F32)
    kern_c = jnp.sum(scaled, axis=0, keepdims=True)

    c_up, c_down, c_far = chan_at(1, 0), chan_at(3, 0), chan_at(2, 0)
    o_me, o_up, o_down, o_far = chan_at(0, 1), chan_at(1, 1), chan_at(3, 1), chan_at(2, 1)
    arrived(2, c_down, top)
    gather(6, c_down, top, up)
    arrived(4, c_up, bot)
    gather(7, c_up, bot, down)

    col0 = pl.multiple_of((me % n_cg) * lanes, lanes)
    rho = jnp.exp(dec[:, pl.ds(col0, lanes)] * (-block / length))
    landed(0)

    def back(i, r):
        b = groups - 1 - i
        src[1, b] = r.astype(BF)
        return rho * (r + dst[0, b].astype(F32))

    lax.fori_loop(0, groups, back, jnp.zeros((16, lanes), F32), unroll=4)
    spread(1)

    arrived(0, o_me, top)
    gather(8, o_me, top, up)
    gather(11, o_me, top, down)

    loads["gk"].wait()
    loads["idft"].wait()
    landed(1)
    unstage(1)
    pspec[pl.ds(0, n_even), :] = (wts[...] * (carry[...] + 0.5 * gspec[pl.ds(0, n_even), :])).astype(BF)
    gc, gsn = gspec[pl.ds(n_even, half), :], gspec[pl.ds(n_even + half, half), :]
    pspec[pl.ds(n_even, half), :] = (inv * (kern_c * gc + kern[...] * gsn)).astype(BF)
    pspec[pl.ds(n_even + half, half), :] = (inv * (kern_c * gsn - kern[...] * gc)).astype(BF)
    gin[...] = grow[...] * mm(idft[...], pspec[...]) + bias[...] * gs[...]
    gval[...] = (gk[...].astype(F32) * gin[...]).astype(BF)

    arrived(1, o_me, bot)
    gather(10, o_me, bot, down)
    gather(9, o_me, bot, up)

    loads["w"].wait()
    loads["tok"].wait()

    def w_of(c):
        return w[pl.ds(pl.multiple_of(c * width, width), width), :]

    acc[...] = mm(tok[chan], w_of(chan))
    arrived(3, c_down, bot)
    acc[...] += mm(tok[c_down], w_of(c_down))
    arrived(5, c_up, top)
    acc[...] += mm(tok[c_up], w_of(c_up))
    acc[...] += mm(tok[o_me], w_of(o_me))

    arrived(8, o_down, top)
    gather(12, o_down, top, up)
    arrived(10, o_up, bot)
    gather(13, o_up, bot, down)

    rs = []

    def reduce_send(i, s, d, target):
        cp = pltpu.make_async_remote_copy(
            src_ref=s, dst_ref=d, send_sem=rs_send.at[i], recv_sem=rs_recv.at[i], device_id=target, device_id_type=MESH,
        )
        cp.start()
        rs.append(cp)

    def reduce_wait(i, r):
        pltpu.make_async_copy(r, r, rs_recv.at[i]).wait()

    def term(p, dy):
        terms[4 * p + dy] = lax.dot_general(gval[...], w_of(chan_at(dy, 1 - p)), NT, preferred_element_type=F32)

    def phase_start(p):
        term(p, 2)
        send_a[p, 0] = terms[4 * p + 2, top].astype(BF)
        send_a[p, 1] = terms[4 * p + 2, bot].astype(BF)
        reduce_send(6 * p, send_a.at[p, 0], got_a.at[p, 0], up)
        reduce_send(6 * p + 1, send_a.at[p, 1], got_a.at[p, 1], down)
        term(p, 1)
        send_p[p, 0] = terms[4 * p + 1, bot].astype(BF)
        reduce_send(6 * p + 2, send_p.at[p, 0], got_b.at[p, 0, bot], up)
        term(p, 3)
        send_p[p, 1] = terms[4 * p + 3, top].astype(BF)
        reduce_send(6 * p + 3, send_p.at[p, 1], got_b.at[p, 1, top], down)

    def phase_middle(p):
        reduce_wait(6 * p, got_a.at[p, 0])
        send_s[p, 0] = (terms[4 * p + 1, top] + got_a[p, 0].astype(F32)).astype(BF)
        reduce_send(6 * p + 4, send_s.at[p, 0], got_b.at[p, 0, top], up)
        reduce_wait(6 * p + 1, got_a.at[p, 1])
        send_s[p, 1] = (terms[4 * p + 3, bot] + got_a[p, 1].astype(F32)).astype(BF)
        reduce_send(6 * p + 5, send_s.at[p, 1], got_b.at[p, 1, bot], down)

    def phase_end(p):
        reduce_wait(6 * p + 2, got_b.at[p, 0, bot])
        reduce_wait(6 * p + 3, got_b.at[p, 1, top])
        reduce_wait(6 * p + 4, got_b.at[p, 0, top])
        reduce_wait(6 * p + 5, got_b.at[p, 1, bot])
        return terms[4 * p] + got_b[p, 0].astype(F32) + got_b[p, 1].astype(F32)

    phase_start(0)

    arrived(6, c_far, top)
    arrived(7, c_far, bot)
    acc[...] += mm(tok[c_far], w_of(c_far))
    arrived(9, o_down, bot)
    acc[...] += mm(tok[o_down], w_of(o_down))
    arrived(11, o_up, top)
    acc[...] += mm(tok[o_up], w_of(o_up))
    arrived(12, o_far, top)
    arrived(13, o_far, bot)
    val[...] = (acc[...] + mm(tok[o_far], w_of(o_far))).astype(BF)
    xin[...] = gk[...].astype(F32) * val[...].astype(F32)
    xspec[...] = mm(dft[...], (xin[...] * grow[...]).astype(BF))
    stage(2, xspec)
    spread(2)

    xc, xs = xspec[pl.ds(n_even, half), :], xspec[pl.ds(n_even + half, half), :]
    gc, gsn = gspec[pl.ds(n_even, half), :], gspec[pl.ds(n_even + half, half), :]
    loads["crosst"].wait()
    part = inv * (
        jnp.sum(gc * xc + gsn * xs, axis=0, keepdims=True)
        + jnp.dot(crosst[...], gsn * xc - gc * xs, precision=EXACT, preferred_element_type=F32)
    )
    part_b = jnp.broadcast_to(jnp.sum(xin[...] * gs[...], axis=0, keepdims=True), (8, width))
    for rg in range(n_rg):
        both = jnp.concatenate([part[8 * rg : 8 * rg + 8], part_b]).astype(BF)
        for cg in range(n_cg):
            src[3, rg * n_cg + cg] = both[:, lanes * cg : lanes * cg + lanes]
    spread(3)

    phase_middle(0)
    phase_start(1)
    term(0, 0)

    landed(2)
    landed(3)

    def fore(b, state):
        z, g_sum, b_sum = state
        x_b, g_b, p_b = dst[2, b].astype(F32), dst[0, b].astype(F32), dst[3, b].astype(F32)
        src[4, b] = z.astype(BF)
        prod = g_b * (z + 0.5 * x_b)
        return rho * (z + x_b), g_sum + prod[0:8] + prod[8:16] + p_b[0:8], b_sum + p_b[8:16]

    eight0 = jnp.zeros((8, lanes), F32)
    _, g_sum, b_sum = lax.fori_loop(0, groups, fore, (jnp.zeros((16, lanes), F32), eight0, eight0), unroll=4)
    spread(4)
    src[5, 0] = jnp.concatenate([g_sum * scale, b_sum]).astype(BF)
    spread(5, True)

    phase_middle(1)
    term(1, 0)
    send_z[...] = phase_end(0).astype(BF)
    reduce_send(12, send_z, got_z, across)

    landed(4)
    unstage(4)
    pspec[pl.ds(0, n_even), :] = (wts[...] * (carry[...] + 0.5 * xspec[pl.ds(0, n_even), :])).astype(BF)
    pspec[pl.ds(n_even, half), :] = (inv * (kern_c * xc - kern[...] * xs)).astype(BF)
    pspec[pl.ds(n_even + half, half), :] = (inv * (kern_c * xs + kern[...] * xc)).astype(BF)
    state = fade[...] * mm(idft[...], pspec[...]) + bias[...] * xin[...]
    mixed_o[...] = (gq[...].astype(F32) * state).astype(BF)
    gqry_o[...] = (cot[...].astype(F32) * state).astype(BF)
    gkey_o[...] = (val[...].astype(F32) * gin[...]).astype(BF)

    acc[...] = phase_end(1)

    landed(5)
    for rg in range(n_rg):
        for cg in range(n_cg):
            d = dst[5, rg * n_cg + cg].astype(F32)
            gf_o[pl.ds(8 * rg, 8), pl.ds(lanes * cg, lanes)] = d[0:8]
            if rg == 0:
                gb_o[:, pl.ds(lanes * cg, lanes)] = d[8:9]

    reduce_wait(12, got_z)
    gtok_o[...] = (acc[...] + got_z[...].astype(F32)).astype(BF)

    for trip in range(6):
        left(trip)
    for cp in ag:
        cp.wait_send()
    for cp in rs:
        cp.wait_send()


def body(tokens, w_value, gate_k, gate_q, filter_weight, decay, skip_bias, cotangent):
    _, block, width = tokens.shape
    seq_size = lax.axis_size("seq")
    groups = seq_size * lax.axis_size("dp")
    chans = lax.axis_size("chan")
    order = filter_weight.shape[0]
    length = block * groups
    half = block // 2
    n_even = 2 * order
    n_spec = n_even + block
    lanes = width * (n_even // 16) // groups
    dft, cross = tables(block, order)
    any_spec = pl.BlockSpec(memory_space=pl.ANY)
    vmem = pl.BlockSpec(memory_space=pltpu.VMEM)
    wide = (block, width)
    outs = pl.pallas_call(
        functools.partial(kernel, seq_size, length),
        out_shape=[jax.ShapeDtypeStruct(wide, BF)] * 4
        + [jax.ShapeDtypeStruct((order, width), F32), jax.ShapeDtypeStruct((1, width), F32)],
        in_specs=[any_spec] * 10 + [vmem] * 2,
        out_specs=[vmem] * 6,
        scratch_shapes=[
            pltpu.VMEM((chans, block, width), BF),
            pltpu.VMEM(w_value.shape, BF),
            pltpu.VMEM(wide, BF),
            pltpu.VMEM(wide, BF),
            pltpu.VMEM((order, width), F32),
            pltpu.VMEM(wide, BF),
            pltpu.VMEM((n_spec, block), BF),
            pltpu.VMEM((block, n_spec), BF),
            pltpu.VMEM((half, order), F32),
            pltpu.VMEM((order, half), F32),
            pltpu.VMEM(wide, F32),
            pltpu.VMEM(wide, F32),
            pltpu.VMEM(wide, F32),
            pltpu.VMEM(wide, F32),
            pltpu.VMEM(wide, F32),
            pltpu.VMEM(wide, BF),
            pltpu.VMEM(wide, BF),
            pltpu.VMEM(wide, F32),
            pltpu.VMEM((n_spec, width), F32),
            pltpu.VMEM((n_spec, width), F32),
            pltpu.VMEM((n_spec, width), BF),
            pltpu.VMEM((half, width), F32),
            pltpu.VMEM((n_even, width), F32),
            pltpu.VMEM((n_even, width), F32),
            pltpu.VMEM((6, groups, 16, lanes), BF),
            pltpu.VMEM((6, groups, 16, lanes), BF),
            pltpu.VMEM((8, block, width), F32),
            pltpu.VMEM((2, 2, block // 2, width), BF),
            pltpu.VMEM((2, 2, block // 2, width), BF),
            pltpu.VMEM((2, 2, block // 2, width), BF),
            pltpu.VMEM(wide, BF),
            pltpu.VMEM((2, 2, block // 2, width), BF),
            pltpu.VMEM((2, 2, block, width), BF),
            pltpu.VMEM(wide, BF),
            pltpu.SemaphoreType.DMA((10,)),
            pltpu.SemaphoreType.DMA((14,)),
            pltpu.SemaphoreType.DMA((14,)),
            pltpu.SemaphoreType.DMA((13,)),
            pltpu.SemaphoreType.DMA((13,)),
            pltpu.SemaphoreType.DMA((6,)),
            pltpu.SemaphoreType.DMA((6,)),
        ],
        compiler_params=pltpu.CompilerParams(
            collective_id=0, has_side_effects=True, vmem_limit_bytes=48 * 2**20
        ),
        name="hyena",
    )(
        tokens[0], w_value, gate_k[0], gate_q[0], filter_weight, cotangent[0],
        jnp.asarray(dft, BF), jnp.asarray(dft.T, BF), jnp.asarray(cross), jnp.asarray(cross.T),
        decay[None], skip_bias[None],
    )
    mixed, gtok, gkey, gqry, gfil, gbias = outs
    return mixed[None], gtok[None], gkey[None], gqry[None], gfil, gbias[0]


def solution(mesh):
    rows = P(None, ("dp", "seq"), "chan")
    cols = P(None, "chan")
    return jax.shard_map(
        body,
        mesh=mesh,
        in_specs=(rows, cols, rows, rows, cols, P("chan"), P("chan"), rows),
        out_specs=(rows, rows, rows, rows, cols, P("chan")),
        check_vma=False,
    )
```

time: 546 us -> 85.4 us (0.16)
  the two profiles are of different devices: /device:TPU:64 before, /device:TPU:8 now
where the time goes in v1:
time: 85.4 us; the launch traced here: 84.9 us
  Pallas kernels  70.7 us (83%)
  local copies, waits for them, and re-layouts  13.6 us (16%)
    pallas_call x1, Pallas kernels, body(): pl.pallas_call(functools.partial(kernel, seq_size, length), out_shape=[ja...  70.7 us
    unnamed x28, local copies, waits for them, and re-layouts  13.6 us

profile of v1, /device:TPU:8, one launch (start us, length us, event | category | flops | bytes accessed | tf_op | source)
XLA Modules:
  0.0 84.9 jit_solution(2032656725252895060)
XLA Ops:
  0.6 0.0 copy-start
  0.6 0.9 %copy-done = bf16[1,256,512]{2,1,0:T(8,128)(2,1)S(1)} copy-done((bf16[1,256,512]{2,1,0:T(8,128)(2,1)S(1)}, bf16[1,256,512]{2,1,0:T(8,128)(2,1)}, u32[]{:S(2)}) %copy-start) | copy-done | bytes 262168
  1.6 0.0 copy-start.1
  1.6 0.9 %copy-done.1 = bf16[1,256,512]{2,1,0:T(8,128)(2,1)S(1)} copy-done((bf16[1,256,512]{2,1,0:T(8,128)(2,1)S(1)}, bf16[1,256,512]{2,1,0:T(8,128)(2,1)}, u32[]{:S(2)}) %copy-start.1) | copy-done | bytes 262168
  2.5 0.0 copy-start.2
  2.5 0.9 %copy-done.2 = bf16[1,256,512]{2,1,0:T(8,128)(2,1)S(1)} copy-done((bf16[1,256,512]{2,1,0:T(8,128)(2,1)S(1)}, bf16[1,256,512]{2,1,0:T(8,128)(2,1)}, u32[]{:S(2)}) %copy-start.2) | copy-done | bytes 262168
  3.5 0.0 copy-start.3
  3.5 0.9 %copy-done.3 = bf16[1,256,512]{2,1,0:T(8,128)(2,1)S(1)} copy-done((bf16[1,256,512]{2,1,0:T(8,128)(2,1)S(1)}, bf16[1,256,512]{2,1,0:T(8,128)(2,1)}, u32[]{:S(2)}) %copy-start.3) | copy-done | bytes 262168
  4.4 0.0 copy-start.4
  4.4 0.9 %copy-done.4 = bf16[256,384]{1,0:T(8,128)(2,1)S(1)} copy-done((bf16[256,384]{1,0:T(8,128)(2,1)S(1)}, bf16[256,384]{1,0:T(8,128)(2,1)}, u32[]{:S(2)}) %copy-start.4) | copy-done | bytes 196632
  5.4 0.0 copy-start.5
  5.4 0.9 %copy-done.5 = bf16[384,256]{1,0:T(8,128)(2,1)S(1)} copy-done((bf16[384,256]{1,0:T(8,128)(2,1)S(1)}, bf16[384,256]{1,0:T(8,128)(2,1)}, u32[]{:S(2)}) %copy-start.5) | copy-done | bytes 196632
  6.3 0.0 copy-start.6
  6.3 0.9 %copy-done.6 = f32[64,512]{1,0:T(8,128)S(1)} copy-done((f32[64,512]{1,0:T(8,128)S(1)}, f32[64,512]{1,0:T(8,128)}, u32[]{:S(2)}) %copy-start.6) | copy-done | bytes 131096
  7.2 0.0 copy-start.7
  7.2 0.8 copy-done.7
  8.0 0.0 copy-start.8
  8.0 0.8 copy-done.8
  8.8 0.0 copy-start.9
  8.8 0.7 copy-done.9
  9.5 0.0 copy-start.10
  9.5 0.7 copy-done.10
  10.2 70.7 %hyena.1 = (bf16[256,512]{1,0:T(8,128)(2,1)S(1)}, bf16[256,512]{1,0:T(8,128)(2,1)S(1)}, bf16[256,512]{1,0:T(8,128)(2,1)S(1)}, bf16[256,512]{1,0:T(8,128)(2,1)S(1...) custom-call(bf16[256,512]{1,0:T(8,128)(2,1)S(1)} %bitcast.11, bf16[4096,512]{1,0:T(8,128)(2,1)} %w_h.1, ...), custom_call_target="tpu_custom_call" | custom-call | tf_op jit(solution)/shard_map/hyena/pallas_call | solution.py:371
  80.9 0.7 copy.24
  81.6 0.7 copy.25
  82.3 0.7 copy.26
  83.0 0.7 copy.27
  83.7 0.7 copy.28
  84.3 0.6 copy.29
Async XLA Ops:
  0.6 1.0 %copy-start = (bf16[1,256,512]{2,1,0:T(8,128)(2,1)S(1)}, bf16[1,256,512]{2,1,0:T(8,128)(2,1)}, u32[]{:S(2)}) copy-start(bf16[1,256,512]{2,1,0:T(8,128)(2,1)} %param.12) | copy-start | bytes 786436
  1.6 0.9 %copy-start.1 = (bf16[1,256,512]{2,1,0:T(8,128)(2,1)S(1)}, bf16[1,256,512]{2,1,0:T(8,128)(2,1)}, u32[]{:S(2)}) copy-start(bf16[1,256,512]{2,1,0:T(8,128)(2,1)} %param.14) | copy-start | bytes 786436
  2.5 0.9 %copy-start.2 = (bf16[1,256,512]{2,1,0:T(8,128)(2,1)S(1)}, bf16[1,256,512]{2,1,0:T(8,128)(2,1)}, u32[]{:S(2)}) copy-start(bf16[1,256,512]{2,1,0:T(8,128)(2,1)} %param.15) | copy-start | bytes 786436
  3.5 0.9 %copy-start.3 = (bf16[1,256,512]{2,1,0:T(8,128)(2,1)S(1)}, bf16[1,256,512]{2,1,0:T(8,128)(2,1)}, u32[]{:S(2)}) copy-start(bf16[1,256,512]{2,1,0:T(8,128)(2,1)} %param.19) | copy-start | bytes 786436
  4.4 0.9 %copy-start.4 = (bf16[256,384]{1,0:T(8,128)(2,1)S(1)}, bf16[256,384]{1,0:T(8,128)(2,1)}, u32[]{:S(2)}) copy-start(bf16[256,384]{1,0:T(8,128)(2,1)} %constant.9.clone.idft_h) | copy-start | bytes 589828
  5.4 0.9 %copy-start.5 = (bf16[384,256]{1,0:T(8,128)(2,1)S(1)}, bf16[384,256]{1,0:T(8,128)(2,1)}, u32[]{:S(2)}) copy-start(bf16[384,256]{1,0:T(8,128)(2,1)} %constant.8.clone.dft_h) | copy-start | bytes 589828
  6.3 0.9 %copy-start.6 = (f32[64,512]{1,0:T(8,128)S(1)}, f32[64,512]{1,0:T(8,128)}, u32[]{:S(2)}) copy-start(f32[64,512]{1,0:T(8,128)} %fw_h.1) | copy-start | bytes 393220
  7.2 0.8 copy-start.7
  8.0 0.8 copy-start.8
  8.8 0.7 copy-start.9
  9.5 0.7 copy-start.10

commit v2 on v1

--- a/solution.py
+++ b/solution.py
@@ -34,9 +34,9 @@
 
 def kernel(
     seq_size, length,
-    tok_h, w_h, gk_h, gq_h, fw_h, cot_h, dft_h, idft_h, cross_h, crosst_h, dec, bias,
+    tok_h, w_h, gk_h, gq_h, fw_h, cot_h, dft_h, idft_h, cross_h, crosst_h, dec_h, bias_h,
     mixed_o, gtok_o, gkey_o, gqry_o, gf_o, gb_o,
-    tok, w, gk, gq, fw, cot, dft, idft, cross, crosst,
+    tok, w, gk, gq, fw, cot, dft, idft, cross, crosst, dec, bias,
     fade, grow, gs, gin, xin, val, gval, acc, gspec, xspec, pspec, kern, wts, carry,
     src, dst, terms, send_a, send_p, send_s, send_z, got_a, got_b, got_z,
     load_sem, ag_send, ag_recv, rs_send, rs_recv, st_send, st_recv,
@@ -71,9 +71,9 @@
 
     loads = {}
     order_of = [
-        ("gq", gq_h, gq), ("cot", cot_h, cot), ("dft", dft_h, dft), ("fw", fw_h, fw), ("cross", cross_h, cross),
+        ("gq", gq_h, gq), ("cot", cot_h, cot), ("dec", dec_h, dec), ("dft", dft_h, dft), ("fw", fw_h, fw), ("cross", cross_h, cross),
         ("gk", gk_h, gk), ("idft", idft_h, idft), ("crosst", crosst_h, crosst), ("w", w_h, w),
-        ("tok", tok_h, tok.at[chan]),
+        ("tok", tok_h, tok.at[chan]), ("bias", bias_h, bias),
     ]
     for i, (name, a, b) in enumerate(order_of):
         loads[name] = pltpu.make_async_copy(a, b, load_sem.at[i])
@@ -92,7 +92,7 @@
 
     top, bot = pl.ds(0, rows), pl.ds(rows, rows)
 
-    ag = []
+    ag = {}
 
     def gather(i, slot, part, target, first=False):
         s = tok_h.at[part] if first else tok.at[slot, part]
@@ -101,18 +101,18 @@
             device_id=target, device_id_type=MESH,
         )
         cp.start()
-        ag.append(cp)
+        ag[i] = cp
 
     def arrived(i, slot, part):
         r = tok.at[slot, part]
         pltpu.make_async_copy(r, r, ag_recv.at[i]).wait()
 
+    def sent(i):
+        ag.pop(i).wait_send()
+
     gather(0, chan, top, across, True)
     gather(2, chan, top, up, True)
     gather(4, chan, bot, down, True)
-    gather(1, chan, bot, across, True)
-    gather(3, chan, bot, up, True)
-    gather(5, chan, top, down, True)
 
     def spread(trip, single=False):
         def one(i, carry_):
@@ -147,6 +147,7 @@
 
     loads["gq"].wait()
     loads["cot"].wait()
+    loads["dec"].wait()
     pos = lax.broadcasted_iota(jnp.int32, (block, width), 0).astype(F32) * (1.0 / length)
     rate = pos * dec[...]
     fade[...] = jnp.exp(-rate)
@@ -157,6 +158,19 @@
     stage(0, gspec)
     spread(0)
 
+    c_up, c_down, c_far = chan_at(1, 0), chan_at(3, 0), chan_at(2, 0)
+    o_me, o_up, o_down, o_far = chan_at(0, 1), chan_at(1, 1), chan_at(3, 1), chan_at(2, 1)
+    sent(2)
+    gather(3, chan, bot, up, True)
+    sent(4)
+    gather(5, chan, top, down, True)
+    arrived(2, c_down, top)
+    gather(6, c_down, top, up)
+    arrived(4, c_up, bot)
+    gather(7, c_up, bot, down)
+    sent(0)
+    gather(1, chan, bot, across, True)
+
     loads["fw"].wait()
     loads["cross"].wait()
     scaled = fw[...] * scale
@@ -167,12 +181,20 @@
     kern[...] = jnp.dot(cross[...], scaled, precision=EXACT, preferred_element_type=F32)
     kern_c = jnp.sum(scaled, axis=0, keepdims=True)
 
-    c_up, c_down, c_far = chan_at(1, 0), chan_at(3, 0), chan_at(2, 0)
-    o_me, o_up, o_down, o_far = chan_at(0, 1), chan_at(1, 1), chan_at(3, 1), chan_at(2, 1)
-    arrived(2, c_down, top)
-    gather(6, c_down, top, up)
-    arrived(4, c_up, bot)
-    gather(7, c_up, bot, down)
+    loads["w"].wait()
+    loads["tok"].wait()
+
+    def w_of(c):
+        return w[pl.ds(pl.multiple_of(c * width, width), width), :]
+
+    acc[...] = mm(tok[chan], w_of(chan))
+    arrived(3, c_down, bot)
+    acc[...] += mm(tok[c_down], w_of(c_down))
+    arrived(5, c_up, top)
+    acc[...] += mm(tok[c_up], w_of(c_up))
+    arrived(0, o_me, top)
+    gather(8, o_me, top, up)
+    gather(11, o_me, top, down)
 
     col0 = pl.multiple_of((me % n_cg) * lanes, lanes)
     rho = jnp.exp(dec[:, pl.ds(col0, lanes)] * (-block / length))
@@ -186,11 +208,14 @@
     lax.fori_loop(0, groups, back, jnp.zeros((16, lanes), F32), unroll=4)
     spread(1)
 
-    arrived(0, o_me, top)
-    gather(8, o_me, top, up)
-    gather(11, o_me, top, down)
+    arrived(8, o_down, top)
+    gather(12, o_down, top, up)
+    arrived(1, o_me, bot)
+    gather(10, o_me, bot, down)
+    gather(9, o_me, bot, up)
 
     loads["gk"].wait()
+    loads["bias"].wait()
     loads["idft"].wait()
     landed(1)
     unstage(1)
@@ -201,28 +226,6 @@
     gin[...] = grow[...] * mm(idft[...], pspec[...]) + bias[...] * gs[...]
     gval[...] = (gk[...].astype(F32) * gin[...]).astype(BF)
 
-    arrived(1, o_me, bot)
-    gather(10, o_me, bot, down)
-    gather(9, o_me, bot, up)
-
-    loads["w"].wait()
-    loads["tok"].wait()
-
-    def w_of(c):
-        return w[pl.ds(pl.multiple_of(c * width, width), width), :]
-
-    acc[...] = mm(tok[chan], w_of(chan))
-    arrived(3, c_down, bot)
-    acc[...] += mm(tok[c_down], w_of(c_down))
-    arrived(5, c_up, top)
-    acc[...] += mm(tok[c_up], w_of(c_up))
-    acc[...] += mm(tok[o_me], w_of(o_me))
-
-    arrived(8, o_down, top)
-    gather(12, o_down, top, up)
-    arrived(10, o_up, bot)
-    gather(13, o_up, bot, down)
-
     rs = []
 
     def reduce_send(i, s, d, target):
@@ -238,20 +241,23 @@
     def term(p, dy):
         terms[4 * p + dy] = lax.dot_general(gval[...], w_of(chan_at(dy, 1 - p)), NT, preferred_element_type=F32)
 
-    def phase_start(p):
+    def far_terms(p):
         term(p, 2)
         send_a[p, 0] = terms[4 * p + 2, top].astype(BF)
         send_a[p, 1] = terms[4 * p + 2, bot].astype(BF)
         reduce_send(6 * p, send_a.at[p, 0], got_a.at[p, 0], up)
         reduce_send(6 * p + 1, send_a.at[p, 1], got_a.at[p, 1], down)
+
+    def near_terms(p):
         term(p, 1)
         send_p[p, 0] = terms[4 * p + 1, bot].astype(BF)
         reduce_send(6 * p + 2, send_p.at[p, 0], got_b.at[p, 0, bot], up)
         term(p, 3)
         send_p[p, 1] = terms[4 * p + 3, top].astype(BF)
         reduce_send(6 * p + 3, send_p.at[p, 1], got_b.at[p, 1, top], down)
-
-    def phase_middle(p):
+        term(p, 0)
+
+    def near_sums(p):
         reduce_wait(6 * p, got_a.at[p, 0])
         send_s[p, 0] = (terms[4 * p + 1, top] + got_a[p, 0].astype(F32)).astype(BF)
         reduce_send(6 * p + 4, send_s.at[p, 0], got_b.at[p, 0, top], up)
@@ -259,18 +265,20 @@
         send_s[p, 1] = (terms[4 * p + 3, bot] + got_a[p, 1].astype(F32)).astype(BF)
         reduce_send(6 * p + 5, send_s.at[p, 1], got_b.at[p, 1, bot], down)
 
-    def phase_end(p):
+    def own_sum(p):
         reduce_wait(6 * p + 2, got_b.at[p, 0, bot])
         reduce_wait(6 * p + 3, got_b.at[p, 1, top])
         reduce_wait(6 * p + 4, got_b.at[p, 0, top])
         reduce_wait(6 * p + 5, got_b.at[p, 1, bot])
         return terms[4 * p] + got_b[p, 0].astype(F32) + got_b[p, 1].astype(F32)
 
-    phase_start(0)
+    arrived(10, o_up, bot)
+    gather(13, o_up, bot, down)
 
     arrived(6, c_far, top)
     arrived(7, c_far, bot)
     acc[...] += mm(tok[c_far], w_of(c_far))
+    acc[...] += mm(tok[o_me], w_of(o_me))
     arrived(9, o_down, bot)
     acc[...] += mm(tok[o_down], w_of(o_down))
     arrived(11, o_up, top)
@@ -282,6 +290,9 @@
     xspec[...] = mm(dft[...], (xin[...] * grow[...]).astype(BF))
     stage(2, xspec)
     spread(2)
+
+    far_terms(0)
+    near_terms(0)
 
     xc, xs = xspec[pl.ds(n_even, half), :], xspec[pl.ds(n_even + half, half), :]
     gc, gsn = gspec[pl.ds(n_even, half), :], gspec[pl.ds(n_even + half, half), :]
@@ -296,31 +307,31 @@
         for cg in range(n_cg):
             src[3, rg * n_cg + cg] = both[:, lanes * cg : lanes * cg + lanes]
     spread(3)
-
-    phase_middle(0)
-    phase_start(1)
-    term(0, 0)
+    near_sums(0)
+    far_terms(1)
 
     landed(2)
-    landed(3)
 
     def fore(b, state):
-        z, g_sum, b_sum = state
-        x_b, g_b, p_b = dst[2, b].astype(F32), dst[0, b].astype(F32), dst[3, b].astype(F32)
+        z, g_sum = state
+        x_b, g_b = dst[2, b].astype(F32), dst[0, b].astype(F32)
         src[4, b] = z.astype(BF)
         prod = g_b * (z + 0.5 * x_b)
-        return rho * (z + x_b), g_sum + prod[0:8] + prod[8:16] + p_b[0:8], b_sum + p_b[8:16]
-
-    eight0 = jnp.zeros((8, lanes), F32)
-    _, g_sum, b_sum = lax.fori_loop(0, groups, fore, (jnp.zeros((16, lanes), F32), eight0, eight0), unroll=4)
+        return rho * (z + x_b), g_sum + prod[0:8] + prod[8:16]
+
+    zero = jnp.zeros((16, lanes), F32)
+    _, g_sum = lax.fori_loop(0, groups, fore, (zero, jnp.zeros((8, lanes), F32)), unroll=4)
     spread(4)
-    src[5, 0] = jnp.concatenate([g_sum * scale, b_sum]).astype(BF)
+
+    landed(3)
+    p_sum = lax.fori_loop(0, groups, lambda b, t: t + dst[3, b].astype(F32), zero, unroll=4)
+    src[5, 0] = jnp.concatenate([(g_sum + p_sum[0:8]) * scale, p_sum[8:16]]).astype(BF)
     spread(5, True)
 
-    phase_middle(1)
-    term(1, 0)
-    send_z[...] = phase_end(0).astype(BF)
+    send_z[...] = own_sum(0).astype(BF)
     reduce_send(12, send_z, got_z, across)
+    near_terms(1)
+    near_sums(1)
 
     landed(4)
     unstage(4)
@@ -332,7 +343,7 @@
     gqry_o[...] = (cot[...].astype(F32) * state).astype(BF)
     gkey_o[...] = (val[...].astype(F32) * gin[...]).astype(BF)
 
-    acc[...] = phase_end(1)
+    acc[...] = own_sum(1)
 
     landed(5)
     for rg in range(n_rg):
@@ -347,10 +358,18 @@
 
     for trip in range(6):
         left(trip)
-    for cp in ag:
+    for cp in ag.values():
         cp.wait_send()
     for cp in rs:
         cp.wait_send()
+
+
+def write_out(*refs):
+    copies = [pltpu.make_async_copy(refs[i], refs[6 + i], refs[12].at[i]) for i in range(6)]
+    for cp in copies:
+        cp.start()
+    for cp in copies:
+        cp.wait()
 
 
 def body(tokens, w_value, gate_k, gate_q, filter_weight, decay, skip_bias, cotangent):
@@ -365,14 +384,14 @@
     n_spec = n_even + block
     lanes = width * (n_even // 16) // groups
     dft, cross = tables(block, order)
-    any_spec = pl.BlockSpec(memory_space=pl.ANY)
+    hbm = pl.BlockSpec(memory_space=pltpu.HBM)
     vmem = pl.BlockSpec(memory_space=pltpu.VMEM)
     wide = (block, width)
     outs = pl.pallas_call(
         functools.partial(kernel, seq_size, length),
         out_shape=[jax.ShapeDtypeStruct(wide, BF)] * 4
         + [jax.ShapeDtypeStruct((order, width), F32), jax.ShapeDtypeStruct((1, width), F32)],
-        in_specs=[any_spec] * 10 + [vmem] * 2,
+        in_specs=[hbm] * 12,
         out_specs=[vmem] * 6,
         scratch_shapes=[
             pltpu.VMEM((chans, block, width), BF),
@@ -385,6 +404,8 @@
             pltpu.VMEM((block, n_spec), BF),
             pltpu.VMEM((half, order), F32),
             pltpu.VMEM((order, half), F32),
+            pltpu.VMEM((1, width), F32),
+            pltpu.VMEM((1, width), F32),
             pltpu.VMEM(wide, F32),
             pltpu.VMEM(wide, F32),
             pltpu.VMEM(wide, F32),
@@ -409,7 +430,7 @@
             pltpu.VMEM((2, 2, block // 2, width), BF),
             pltpu.VMEM((2, 2, block, width), BF),
             pltpu.VMEM(wide, BF),
-            pltpu.SemaphoreType.DMA((10,)),
+            pltpu.SemaphoreType.DMA((12,)),
             pltpu.SemaphoreType.DMA((14,)),
             pltpu.SemaphoreType.DMA((14,)),
             pltpu.SemaphoreType.DMA((13,)),
@@ -418,7 +439,7 @@
             pltpu.SemaphoreType.DMA((6,)),
         ],
         compiler_params=pltpu.CompilerParams(
-            collective_id=0, has_side_effects=True, vmem_limit_bytes=48 * 2**20
+            collective_id=0, has_side_effects=True, vmem_limit_bytes=60 * 2**20
         ),
         name="hyena",
     )(
@@ -426,7 +447,15 @@
         jnp.asarray(dft, BF), jnp.asarray(dft.T, BF), jnp.asarray(cross), jnp.asarray(cross.T),
         decay[None], skip_bias[None],
     )
-    mixed, gtok, gkey, gqry, gfil, gbias = outs
+    mixed, gtok, gkey, gqry, gfil, gbias = pl.pallas_call(
+        write_out,
+        out_shape=[jax.ShapeDtypeStruct(o.shape, o.dtype) for o in outs],
+        in_specs=[vmem] * 6,
+        out_specs=[hbm] * 6,
+        scratch_shapes=[pltpu.SemaphoreType.DMA((6,))],
+        compiler_params=pltpu.CompilerParams(vmem_limit_bytes=60 * 2**20),
+        name="write_out",
+    )(*outs)
     return mixed[None], gtok[None], gkey[None], gqry[None], gfil, gbias[0]
 
 

time: 85.4 us -> 68.9 us (0.81)
  the two profiles are of different devices: /device:TPU:8 before, /device:TPU:14 now
where the time goes in v2:
time: 68.9 us; the launch traced here: 68.8 us
  Pallas kernels  68.1 us (99%)
    pallas_call x1, Pallas kernels, body(): pl.pallas_call(functools.partial(kernel, seq_size, length), out_shape=[ja...  65.8 us
    pallas_call x1, Pallas kernels, body(): pl.pallas_call(write_out, out_shape=[jax.ShapeDtypeStruct(o.shape, o.dtyp...  2.28 us

profile of v2, /device:TPU:14, one launch (start us, length us, event | category | flops | bytes accessed | tf_op | source)
XLA Modules:
  0.0 68.8 jit_solution(9517007586852145381)
XLA Ops:
  0.6 65.8 %hyena.1 = (bf16[256,512]{1,0:T(8,128)(2,1)}, bf16[256,512]{1,0:T(8,128)(2,1)}, bf16[256,512]{1,0:T(8,128)(2,1)}, bf16[256,512]{1,0:T(8,128)(2,1)}, f32[64,512]{1,0:T(8,128)}, /*index=5*/f32[1,512]{1,0:T(1,128)}) custom-call(bf16[256,512]{1,0:T(8,128)(2,1)} %bitcast.11, bf16[4096,512]{1,0:T(8,128)(2,1)} %w_h.1, bf16[256,512]{1,0:T(8,128)(2,1)} %bitcast.12, ...), custom_call_target="tpu_custom_call" | custom-call | tf_op jit(solution)/shard_map/hyena/pallas_call | solution.py:390
  66.5 2.3 %write_out.1 = (bf16[256,512]{1,0:T(8,128)(2,1)}, bf16[256,512]{1,0:T(8,128)(2,1)}, bf16[256,512]{1,0:T(8,128)(2,1)}, bf16[256,512]{1,0:T(8,128)(2,1)}, f32[64,512]{1,0:T(8,128)}, /*index=5*/f32[1,512]{1,0:T(1,128)}) custom-call(bf16[256,512]{1,0:T(8,128)(2,1)} %get-tuple-element.18.refs_0_, bf16[256,512]{1,0:T(8,128)(2,1)} %get-tuple-element.19.refs_1_, ...), custom_call_target="tpu_custom_call" | custom-call | tf_op jit(solution)/shard_map/write_out/pallas_call | solution.py:450

commit v3 on v2

--- a/solution.py
+++ b/solution.py
@@ -39,7 +39,7 @@
     tok, w, gk, gq, fw, cot, dft, idft, cross, crosst, dec, bias,
     fade, grow, gs, gin, xin, val, gval, acc, gspec, xspec, pspec, kern, wts, carry,
     src, dst, terms, send_a, send_p, send_s, send_z, got_a, got_b, got_z,
-    load_sem, ag_send, ag_recv, rs_send, rs_recv, st_send, st_recv,
+    load_sem, ag_send, ag_recv, rs_send, rs_recv, st_send, st_recv, hop_send, hop_recv,
 ):
     block, width = gk.shape
     rows = block // 2
@@ -69,6 +69,15 @@
         b = (me + i) % groups
         return b, (b // seq_size, b % seq_size, chan)
 
+    barrier = pltpu.get_barrier_semaphore()
+    for target in (up, down, across):
+        pl.semaphore_signal(barrier, inc=1, device_id=target, device_id_type=MESH)
+
+    def greet(i, carry_):
+        pl.semaphore_signal(barrier, inc=1, device_id=peer(i)[1], device_id_type=MESH)
+        return carry_
+
+    lax.fori_loop(1, groups, greet, 0)
     loads = {}
     order_of = [
         ("gq", gq_h, gq), ("cot", cot_h, cot), ("dec", dec_h, dec), ("dft", dft_h, dft), ("fw", fw_h, fw), ("cross", cross_h, cross),
@@ -78,16 +87,11 @@
     for i, (name, a, b) in enumerate(order_of):
         loads[name] = pltpu.make_async_copy(a, b, load_sem.at[i])
         loads[name].start()
-
-    barrier = pltpu.get_barrier_semaphore()
-    for target in (up, down, across):
-        pl.semaphore_signal(barrier, inc=1, device_id=target, device_id_type=MESH)
-
-    def greet(i, carry_):
-        pl.semaphore_signal(barrier, inc=1, device_id=peer(i)[1], device_id_type=MESH)
-        return carry_
-
-    lax.fori_loop(1, groups, greet, 0)
+    def stage(trip, ref):
+        for rg in range(n_rg):
+            for cg in range(n_cg):
+                src[trip, rg * n_cg + cg] = ref[pl.ds(16 * rg, 16), pl.ds(lanes * cg, lanes)].astype(BF)
+
     pl.semaphore_wait(barrier, groups + 2)
 
     top, bot = pl.ds(0, rows), pl.ds(rows, rows)
@@ -114,10 +118,10 @@
     gather(2, chan, top, up, True)
     gather(4, chan, bot, down, True)
 
-    def spread(trip, single=False):
+    def spread(trip):
         def one(i, carry_):
             b, target = peer(i)
-            s = src.at[trip, 0] if single else src.at[trip, b]
+            s = src.at[trip, b]
             pltpu.make_async_remote_copy(
                 src_ref=s, dst_ref=dst.at[trip, me], send_sem=st_send.at[trip], recv_sem=st_recv.at[trip],
                 device_id=target, device_id_type=MESH,
@@ -125,7 +129,35 @@
             return carry_
 
         lax.fori_loop(1, groups, one, 0, unroll=True)
-        dst[trip, me] = src[trip, 0] if single else src[trip, me]
+        dst[trip, me] = src[trip, me]
+
+    side = 4
+    at_x, at_z = seq % side, seq // side
+
+    def place(b):
+        return (b // seq_size) * seq_size + (b % side) * side + (b % seq_size) // side
+
+    def hop(step, s, d, target):
+        pltpu.make_async_remote_copy(
+            src_ref=s, dst_ref=d, send_sem=hop_send.at[step], recv_sem=hop_recv.at[step],
+            device_id=target, device_id_type=MESH,
+        ).start()
+
+    def hop_wait(step, n):
+        r = dst.at[5, pl.ds(0, n)]
+        pltpu.make_async_copy(r, r, hop_recv.at[step]).wait()
+
+    def hop_left(step, n):
+        r = dst.at[5, pl.ds(0, n)]
+        pltpu.make_async_copy(r, r, hop_send.at[step]).wait()
+
+    def z_peer(i):
+        return (dp, ((at_z + i) % side) * side + at_x, chan)
+
+    def x_peer(i):
+        return (dp, at_z * side + (at_x + i) % side, chan)
+
+    core_peer = (1 - dp, seq, chan)
 
     def landed(trip):
         r = dst.at[trip, pl.ds(0, groups - 1)]
@@ -134,11 +166,6 @@
     def left(trip):
         r = src.at[trip, pl.ds(0, groups - 1)]
         pltpu.make_async_copy(r, r, st_send.at[trip]).wait()
-
-    def stage(trip, ref):
-        for rg in range(n_rg):
-            for cg in range(n_cg):
-                src[trip, rg * n_cg + cg] = ref[pl.ds(16 * rg, 16), pl.ds(lanes * cg, lanes)].astype(BF)
 
     def unstage(trip):
         for rg in range(n_rg):
@@ -157,6 +184,16 @@
     gspec[...] = mm(dft[...], (gs[...] * fade[...]).astype(BF))
     stage(0, gspec)
     spread(0)
+    loads["fw"].wait()
+    loads["cross"].wait()
+    scaled = fw[...] * scale
+    for rg in range(n_rg):
+        eight = scaled[8 * rg : 8 * rg + 8]
+        wts[pl.ds(16 * rg, 8), :] = eight
+        wts[pl.ds(16 * rg + 8, 8), :] = eight
+    kern[...] = jnp.dot(cross[...], scaled, precision=EXACT, preferred_element_type=F32)
+    kern_c = jnp.sum(scaled, axis=0, keepdims=True)
+
 
     c_up, c_down, c_far = chan_at(1, 0), chan_at(3, 0), chan_at(2, 0)
     o_me, o_up, o_down, o_far = chan_at(0, 1), chan_at(1, 1), chan_at(3, 1), chan_at(2, 1)
@@ -171,16 +208,6 @@
     sent(0)
     gather(1, chan, bot, across, True)
 
-    loads["fw"].wait()
-    loads["cross"].wait()
-    scaled = fw[...] * scale
-    for rg in range(n_rg):
-        eight = scaled[8 * rg : 8 * rg + 8]
-        wts[pl.ds(16 * rg, 8), :] = eight
-        wts[pl.ds(16 * rg + 8, 8), :] = eight
-    kern[...] = jnp.dot(cross[...], scaled, precision=EXACT, preferred_element_type=F32)
-    kern_c = jnp.sum(scaled, axis=0, keepdims=True)
-
     loads["w"].wait()
     loads["tok"].wait()
 
@@ -196,27 +223,30 @@
     gather(8, o_me, top, up)
     gather(11, o_me, top, down)
 
-    col0 = pl.multiple_of((me % n_cg) * lanes, lanes)
-    rho = jnp.exp(dec[:, pl.ds(col0, lanes)] * (-block / length))
-    landed(0)
-
-    def back(i, r):
-        b = groups - 1 - i
-        src[1, b] = r.astype(BF)
-        return rho * (r + dst[0, b].astype(F32))
-
-    lax.fori_loop(0, groups, back, jnp.zeros((16, lanes), F32), unroll=4)
-    spread(1)
-
+    loads["gk"].wait()
+    loads["bias"].wait()
+    loads["idft"].wait()
     arrived(8, o_down, top)
     gather(12, o_down, top, up)
     arrived(1, o_me, bot)
     gather(10, o_me, bot, down)
     gather(9, o_me, bot, up)
 
-    loads["gk"].wait()
-    loads["bias"].wait()
-    loads["idft"].wait()
+    col0 = pl.multiple_of((me % n_cg) * lanes, lanes)
+    rho = jnp.exp(dec[:, pl.ds(col0, lanes)] * (-block / length))
+    landed(0)
+
+    def back(i, r):
+        b = groups - 1 - i
+        src[1, b] = r.astype(BF)
+        return rho * (r + dst[0, b].astype(F32))
+
+    lax.fori_loop(0, groups, back, jnp.zeros((16, lanes), F32), unroll=4)
+    spread(1)
+
+    arrived(10, o_up, bot)
+    gather(13, o_up, bot, down)
+
     landed(1)
     unstage(1)
     pspec[pl.ds(0, n_even), :] = (wts[...] * (carry[...] + 0.5 * gspec[pl.ds(0, n_even), :])).astype(BF)
@@ -271,9 +301,6 @@
         reduce_wait(6 * p + 4, got_b.at[p, 0, top])
         reduce_wait(6 * p + 5, got_b.at[p, 1, bot])
         return terms[4 * p] + got_b[p, 0].astype(F32) + got_b[p, 1].astype(F32)
-
-    arrived(10, o_up, bot)
-    gather(13, o_up, bot, down)
 
     arrived(6, c_far, top)
     arrived(7, c_far, bot)
@@ -326,12 +353,19 @@
     landed(3)
     p_sum = lax.fori_loop(0, groups, lambda b, t: t + dst[3, b].astype(F32), zero, unroll=4)
     src[5, 0] = jnp.concatenate([(g_sum + p_sum[0:8]) * scale, p_sum[8:16]]).astype(BF)
-    spread(5, True)
+    dst[5, place(me)] = src[5, 0]
+    for i in range(1, side):
+        hop(0, src.at[5, 0], dst.at[5, place(me)], z_peer(i))
 
     send_z[...] = own_sum(0).astype(BF)
     reduce_send(12, send_z, got_z, across)
     near_terms(1)
     near_sums(1)
+
+    hop_wait(0, side - 1)
+    mine = pl.ds(dp * seq_size + at_x * side, side)
+    for i in range(1, side):
+        hop(1, dst.at[5, mine], dst.at[5, mine], x_peer(i))
 
     landed(4)
     unstage(4)
@@ -345,19 +379,24 @@
 
     acc[...] = own_sum(1)
 
-    landed(5)
+    hop_wait(1, side * (side - 1))
+    half_of = pl.ds(dp * seq_size, seq_size)
+    hop(2, dst.at[5, half_of], dst.at[5, half_of], core_peer)
+    hop_wait(2, seq_size)
     for rg in range(n_rg):
         for cg in range(n_cg):
-            d = dst[5, rg * n_cg + cg].astype(F32)
+            d = dst[5, place(rg * n_cg + cg)].astype(F32)
             gf_o[pl.ds(8 * rg, 8), pl.ds(lanes * cg, lanes)] = d[0:8]
             if rg == 0:
                 gb_o[:, pl.ds(lanes * cg, lanes)] = d[8:9]
-
     reduce_wait(12, got_z)
     gtok_o[...] = (acc[...] + got_z[...].astype(F32)).astype(BF)
 
-    for trip in range(6):
+    for trip in range(5):
         left(trip)
+    hop_left(0, side - 1)
+    hop_left(1, side * (side - 1))
+    hop_left(2, seq_size)
     for cp in ag.values():
         cp.wait_send()
     for cp in rs:
@@ -437,6 +476,8 @@
             pltpu.SemaphoreType.DMA((13,)),
             pltpu.SemaphoreType.DMA((6,)),
             pltpu.SemaphoreType.DMA((6,)),
+            pltpu.SemaphoreType.DMA((6,)),
+            pltpu.SemaphoreType.DMA((6,)),
         ],
         compiler_params=pltpu.CompilerParams(
             collective_id=0, has_side_effects=True, vmem_limit_bytes=60 * 2**20

time: 68.9 us -> 63.5 us (0.922)
  the two profiles are of different devices: /device:TPU:14 before, /device:TPU:64 now
where the time goes in v3:
time: 63.5 us; the launch traced here: 63.4 us
  Pallas kernels  62.7 us (99%)
  between operations  0.64 us (1%)
    pallas_call x1, Pallas kernels, body(): pl.pallas_call(functools.partial(kernel, seq_size, length), out_shape=[ja...  60.5 us
    pallas_call x1, Pallas kernels, body(): pl.pallas_call(write_out, out_shape=[jax.ShapeDtypeStruct(o.shape, o.dtyp...  2.28 us

profile of v3, /device:TPU:64, one launch (start us, length us, event | category | flops | bytes accessed | tf_op | source)
XLA Modules:
  0.0 63.4 jit_solution(18385224327515828677)
XLA Ops:
  0.6 60.5 %hyena.1 = (bf16[256,512]{1,0:T(8,128)(2,1)}, bf16[256,512]{1,0:T(8,128)(2,1)}, bf16[256,512]{1,0:T(8,128)(2,1)}, bf16[256,512]{1,0:T(8,128)(2,1)}, f32[64,512]{1,0:T(8,128)}, /*index=5*/f32[1,512]{1,0:T(1,128)}) custom-call(bf16[256,512]{1,0:T(8,128)(2,1)} %bitcast.11, bf16[4096,512]{1,0:T(8,128)(2,1)} %w_h.1, bf16[256,512]{1,0:T(8,128)(2,1)} %bitcast.12, ...), custom_call_target="tpu_custom_call" | custom-call | tf_op jit(solution)/shard_map/hyena/pallas_call | solution.py:429
  61.1 2.3 %write_out.1 = (bf16[256,512]{1,0:T(8,128)(2,1)}, bf16[256,512]{1,0:T(8,128)(2,1)}, bf16[256,512]{1,0:T(8,128)(2,1)}, bf16[256,512]{1,0:T(8,128)(2,1)}, f32[64,512]{1,0:T(8,128)}, /*index=5*/f32[1,512]{1,0:T(1,128)}) custom-call(bf16[256,512]{1,0:T(8,128)(2,1)} %get-tuple-element.18.refs_0_, bf16[256,512]{1,0:T(8,128)(2,1)} %get-tuple-element.19.refs_1_, ...), custom_call_target="tpu_custom_call" | custom-call | tf_op jit(solution)/shard_map/write_out/pallas_call | solution.py:491

commit v4 on v3

--- a/solution.py
+++ b/solution.py
@@ -241,7 +241,7 @@
         src[1, b] = r.astype(BF)
         return rho * (r + dst[0, b].astype(F32))
 
-    lax.fori_loop(0, groups, back, jnp.zeros((16, lanes), F32), unroll=4)
+    lax.fori_loop(0, groups, back, jnp.zeros((16, lanes), F32), unroll=8)
     spread(1)
 
     arrived(10, o_up, bot)
@@ -347,11 +347,11 @@
         return rho * (z + x_b), g_sum + prod[0:8] + prod[8:16]
 
     zero = jnp.zeros((16, lanes), F32)
-    _, g_sum = lax.fori_loop(0, groups, fore, (zero, jnp.zeros((8, lanes), F32)), unroll=4)
+    _, g_sum = lax.fori_loop(0, groups, fore, (zero, jnp.zeros((8, lanes), F32)), unroll=8)
     spread(4)
 
     landed(3)
-    p_sum = lax.fori_loop(0, groups, lambda b, t: t + dst[3, b].astype(F32), zero, unroll=4)
+    p_sum = jnp.sum(dst[3].astype(F32), axis=0)
     src[5, 0] = jnp.concatenate([(g_sum + p_sum[0:8]) * scale, p_sum[8:16]]).astype(BF)
     dst[5, place(me)] = src[5, 0]
     for i in range(1, side):

time: 63.5 us -> 63.5 us (level)
  no operation moved by 1% of the time
where the time goes in v4:
time: 63.5 us; the launch traced here: 63.4 us
  Pallas kernels  62.7 us (99%)
  between operations  0.64 us (1%)
    pallas_call x1, Pallas kernels, body(): pl.pallas_call(functools.partial(kernel, seq_size, length), out_shape=[ja...  60.4 us
    pallas_call x1, Pallas kernels, body(): pl.pallas_call(write_out, out_shape=[jax.ShapeDtypeStruct(o.shape, o.dtyp...  2.28 us

profile of v4, /device:TPU:64, one launch (start us, length us, event | category | flops | bytes accessed | tf_op | source)
XLA Modules:
  0.0 63.4 jit_solution(10488850843167517065)
XLA Ops:
  0.6 60.4 %hyena.1 = (bf16[256,512]{1,0:T(8,128)(2,1)}, bf16[256,512]{1,0:T(8,128)(2,1)}, bf16[256,512]{1,0:T(8,128)(2,1)}, bf16[256,512]{1,0:T(8,128)(2,1)}, f32[64,512]{1,0:T(8,128)}, /*index=5*/f32[1,512]{1,0:T(1,128)}) custom-call(bf16[256,512]{1,0:T(8,128)(2,1)} %bitcast.11, bf16[4096,512]{1,0:T(8,128)(2,1)} %w_h.1, bf16[256,512]{1,0:T(8,128)(2,1)} %bitcast.12, ...), custom_call_target="tpu_custom_call" | custom-call | tf_op jit(solution)/shard_map/hyena/pallas_call | solution.py:429
  61.1 2.3 %write_out.1 = (bf16[256,512]{1,0:T(8,128)(2,1)}, bf16[256,512]{1,0:T(8,128)(2,1)}, bf16[256,512]{1,0:T(8,128)(2,1)}, bf16[256,512]{1,0:T(8,128)(2,1)}, f32[64,512]{1,0:T(8,128)}, /*index=5*/f32[1,512]{1,0:T(1,128)}) custom-call(bf16[256,512]{1,0:T(8,128)(2,1)} %get-tuple-element.18.refs_0_, bf16[256,512]{1,0:T(8,128)(2,1)} %get-tuple-element.19.refs_1_, ...), custom_call_target="tpu_custom_call" | custom-call | tf_op jit(solution)/shard_map/write_out/pallas_call | solution.py:491

commit v5 on v4

--- a/solution.py
+++ b/solution.py
@@ -358,7 +358,8 @@
         hop(0, src.at[5, 0], dst.at[5, place(me)], z_peer(i))
 
     send_z[...] = own_sum(0).astype(BF)
-    reduce_send(12, send_z, got_z, across)
+    reduce_send(12, send_z.at[top], got_z.at[top], across)
+    reduce_send(13, send_z.at[bot], got_z.at[bot], across)
     near_terms(1)
     near_sums(1)
 
@@ -389,8 +390,9 @@
             gf_o[pl.ds(8 * rg, 8), pl.ds(lanes * cg, lanes)] = d[0:8]
             if rg == 0:
                 gb_o[:, pl.ds(lanes * cg, lanes)] = d[8:9]
-    reduce_wait(12, got_z)
-    gtok_o[...] = (acc[...] + got_z[...].astype(F32)).astype(BF)
+    for i, part in ((12, top), (13, bot)):
+        reduce_wait(i, got_z.at[part])
+        gtok_o[part, :] = (acc[part, :] + got_z[part, :].astype(F32)).astype(BF)
 
     for trip in range(5):
         left(trip)
@@ -472,8 +474,8 @@
             pltpu.SemaphoreType.DMA((12,)),
             pltpu.SemaphoreType.DMA((14,)),
             pltpu.SemaphoreType.DMA((14,)),
-            pltpu.SemaphoreType.DMA((13,)),
-            pltpu.SemaphoreType.DMA((13,)),
+            pltpu.SemaphoreType.DMA((14,)),
+            pltpu.SemaphoreType.DMA((14,)),
             pltpu.SemaphoreType.DMA((6,)),
             pltpu.SemaphoreType.DMA((6,)),
             pltpu.SemaphoreType.DMA((6,)),

time: 63.5 us -> 63.5 us (level)
  no operation moved by 1% of the time
where the time goes in v5:
time: 63.5 us; the launch traced here: 63.4 us
  Pallas kernels  62.7 us (99%)
  between operations  0.64 us (1%)
    pallas_call x1, Pallas kernels, body(): pl.pallas_call(functools.partial(kernel, seq_size, length), out_shape=[ja...  60.4 us
    pallas_call x1, Pallas kernels, body(): pl.pallas_call(write_out, out_shape=[jax.ShapeDtypeStruct(o.shape, o.dtyp...  2.28 us

profile of v5, /device:TPU:64, one launch (start us, length us, event | category | flops | bytes accessed | tf_op | source)
XLA Modules:
  0.0 63.4 jit_solution(2918015264424104993)
XLA Ops:
  0.6 60.4 %hyena.1 = (bf16[256,512]{1,0:T(8,128)(2,1)}, bf16[256,512]{1,0:T(8,128)(2,1)}, bf16[256,512]{1,0:T(8,128)(2,1)}, bf16[256,512]{1,0:T(8,128)(2,1)}, f32[64,512]{1,0:T(8,128)}, /*index=5*/f32[1,512]{1,0:T(1,128)}) custom-call(bf16[256,512]{1,0:T(8,128)(2,1)} %bitcast.11, bf16[4096,512]{1,0:T(8,128)(2,1)} %w_h.1, bf16[256,512]{1,0:T(8,128)(2,1)} %bitcast.12, ...), custom_call_target="tpu_custom_call" | custom-call | tf_op jit(solution)/shard_map/hyena/pallas_call | solution.py:431
  61.1 2.3 %write_out.1 = (bf16[256,512]{1,0:T(8,128)(2,1)}, bf16[256,512]{1,0:T(8,128)(2,1)}, bf16[256,512]{1,0:T(8,128)(2,1)}, bf16[256,512]{1,0:T(8,128)(2,1)}, f32[64,512]{1,0:T(8,128)}, /*index=5*/f32[1,512]{1,0:T(1,128)}) custom-call(bf16[256,512]{1,0:T(8,128)(2,1)} %get-tuple-element.18.refs_0_, bf16[256,512]{1,0:T(8,128)(2,1)} %get-tuple-element.19.refs_1_, ...), custom_call_target="tpu_custom_call" | custom-call | tf_op jit(solution)/shard_map/write_out/pallas_call | solution.py:493
